TPU v7x, 128 devices: a whole 4x4x4 slice. The times are simulated.
128 devices in a mesh: fsdp: 8 (over x_hi, z), context: 8 (over x_lo, y), tensor: 2 (over core).
Axes of the slice: x: 4 (x_hi: 2, x_lo: 2; x = x_hi * 2 + x_lo), y: 4, z: 4, core: 2. Of those that a mesh axis runs over, the one named last changes fastest.
Arguments:
- stream: bfloat16 [1024, 16, 1024], P('context', 'fsdp'), may hold values from -6 to 6
- lengths: int32 [16], P('fsdp'), may hold values from 256 to 1024, as said below
- query_weight: bfloat16 [1024, 1024], P(('fsdp', 'context'), 'tensor'), may hold values from -0.1875 to 0.1875
- query_bias: bfloat16 [1024], P('tensor'), may hold values from -1.75 to 1.75
- key_weight: bfloat16 [1024, 1024], P(('fsdp', 'context'), 'tensor'), may hold values from -0.1875 to 0.1875
- value_weight: bfloat16 [1024, 1024], P(('fsdp', 'context'), 'tensor'), may hold values from -0.1875 to 0.1875
- value_bias: bfloat16 [1024], P('tensor'), may hold values from -0.1875 to 0.1875
- output_weight: bfloat16 [1024, 1024], P('tensor', ('fsdp', 'context')), may hold values from -3 to 3
- output_bias: bfloat16 [1024], P(('fsdp', 'context')), may hold values from -1.75 to 1.75
- first_gain: bfloat16 [1024], P(('fsdp', 'context')), may hold values from 0.5 to 1.5
- first_shift: bfloat16 [1024], P(('fsdp', 'context')), may hold values from -1.75 to 1.75
- inner_weight: bfloat16 [1024, 4096], P(('fsdp', 'context'), 'tensor'), may hold values from -0.1875 to 0.1875
- inner_bias: bfloat16 [4096], P('tensor'), may hold values from -1.75 to 1.75
- outer_weight: bfloat16 [4096, 1024], P('tensor', ('fsdp', 'context')), may hold values from -0.09375 to 0.09375
- outer_bias: bfloat16 [1024], P(('fsdp', 'context')), may hold values from -1.75 to 1.75
- second_gain: bfloat16 [1024], P(('fsdp', 'context')), may hold values from 0.5 to 1.5
- second_shift: bfloat16 [1024], P(('fsdp', 'context')), may hold values from -1.75 to 1.75
- cotangent: bfloat16 [1024, 16, 1024], P('context', 'fsdp'), may hold values from -6 to 6
Outputs:
- result: bfloat16 [1024, 16, 1024], P('context', 'fsdp')
- stream_grad: float32 [1024, 16, 1024], P('context', 'fsdp')
- grad_query_weight: float32 [1024, 1024], P(('fsdp', 'context'), 'tensor')
- grad_query_bias: float32 [1024], P('tensor')
- grad_key_weight: float32 [1024, 1024], P(('fsdp', 'context'), 'tensor')
- grad_value_weight: float32 [1024, 1024], P(('fsdp', 'context'), 'tensor')
- grad_value_bias: float32 [1024], P('tensor')
- grad_output_weight: float32 [1024, 1024], P('tensor', ('fsdp', 'context'))
- grad_output_bias: float32 [1024], P(('fsdp', 'context'))
- grad_first_gain: float32 [1024], P(('fsdp', 'context'))
- grad_first_shift: float32 [1024], P(('fsdp', 'context'))
- grad_inner_weight: float32 [1024, 4096], P(('fsdp', 'context'), 'tensor')
- grad_inner_bias: float32 [4096], P('tensor')
- grad_outer_weight: float32 [4096, 1024], P('tensor', ('fsdp', 'context'))
- grad_outer_bias: float32 [1024], P(('fsdp', 'context'))
- grad_second_gain: float32 [1024], P(('fsdp', 'context'))
- grad_second_shift: float32 [1024], P(('fsdp', 'context'))
- root_squares: float32 [2, 3], replicated
Inputs may be any that keep to these rules, and one draw needn't show every extreme that they name: `lengths`: among the 2 sequences of each index of fsdp, one, drawn from the seed, has more than 896 valid slots.
All inputs are finite; a program needn't handle non-finite values.
Results may differ from a plain program's by a relative error of at most 0.03.
Values may be sent and summed in bfloat16 or wider, within the bound.
A program may use at most 192 MiB of HBM per device.

v0:
```python
import math

import jax
import jax.numpy as jnp
from jax import lax
from jax.sharding import PartitionSpec as P

HEAD = 64
LAYERS = 2


def gelu_tanh(argument):
    return (
        0.5
        * argument
        * (
            1.0
            + jnp.tanh(0.7978845608028654 * (argument + 0.044715 * argument * argument * argument))
        )
    )


def normalize(hidden, gain_vector, shift_term):
    centre = hidden - jnp.mean(hidden, -1, keepdims=True)
    inverse = lax.rsqrt(jnp.mean(centre * centre, -1, keepdims=True) + 1e-05)
    normed = centre * inverse
    return (normed * gain_vector + shift_term, normed, inverse)


def normalize_back(grad_out, normed, inverse, gain_vector):
    scaled = grad_out * gain_vector
    return inverse * (
        scaled
        - jnp.mean(scaled, -1, keepdims=True)
        - normed * jnp.mean(scaled * normed, -1, keepdims=True)
    )


def body(
    stream,
    lengths,
    query_weight,
    query_bias,
    key_weight,
    value_weight,
    value_bias,
    output_weight,
    output_bias,
    first_gain,
    first_shift,
    inner_weight,
    inner_bias,
    outer_weight,
    outer_bias,
    second_gain,
    second_shift,
    cotangent,
):
    slot_count, seq_count, model_width = stream.shape
    row_count = slot_count * seq_count
    heads_here = query_weight.shape[1] // HEAD
    scale_factor = 1.0 / math.sqrt(HEAD)
    position = lax.axis_index("context") * slot_count + jnp.arange(slot_count, dtype=jnp.int32)
    row_live = (position[:, None] < lengths[None, :]).astype(jnp.float32).reshape(row_count, 1)

    def fetch_weights():
        return (
            lax.all_gather(query_weight, ("fsdp", "context"), axis=0, tiled=True),
            lax.all_gather(key_weight, ("fsdp", "context"), axis=0, tiled=True),
            lax.all_gather(value_weight, ("fsdp", "context"), axis=0, tiled=True),
            lax.all_gather(output_weight, ("fsdp", "context"), axis=1, tiled=True),
            lax.all_gather(inner_weight, ("fsdp", "context"), axis=0, tiled=True),
            lax.all_gather(outer_weight, ("fsdp", "context"), axis=1, tiled=True),
            lax.all_gather(output_bias, ("fsdp", "context"), axis=0, tiled=True),
            lax.all_gather(outer_bias, ("fsdp", "context"), axis=0, tiled=True),
            lax.all_gather(first_gain, ("fsdp", "context"), axis=0, tiled=True),
            lax.all_gather(first_shift, ("fsdp", "context"), axis=0, tiled=True),
            lax.all_gather(second_gain, ("fsdp", "context"), axis=0, tiled=True),
            lax.all_gather(second_shift, ("fsdp", "context"), axis=0, tiled=True),
        )

    def join_partial(partial_value):
        return lax.psum(partial_value.astype(jnp.bfloat16), "tensor").astype(jnp.float32)

    def join_back(partial_value):
        return lax.psum(partial_value.astype(jnp.bfloat16), "tensor").astype(jnp.float32)

    def score_block(queries, keys_all):
        key_live = jnp.arange(keys_all.shape[0], dtype=jnp.int32)[None, :] < lengths[:, None]
        raw = jnp.einsum("rshd,kshd->shrk", queries, keys_all, preferred_element_type=jnp.float32)
        return jnp.where(key_live[:, None, None, :], raw * scale_factor, -1e30)

    def head_split(matrix):
        return matrix.reshape(slot_count, seq_count, heads_here, HEAD)

    def backward_attn(grad_middle, stored, weights, grad_sums):
        (
            query_full,
            key_full,
            value_full,
            output_full,
            inner_full,
            outer_full,
            bias_output,
            bias_outer,
            gain_first,
            shift_first,
            gain_second,
            shift_second,
        ) = weights
        (
            flat_in,
            queries,
            keys_all,
            values_all,
            log_total,
            mixed,
            normed_first,
            inverse_first,
            middle_low,
            inner_pre,
            normed_second,
            inverse_second,
        ) = stored
        grad_sums = list(grad_sums)
        grad_sums[8] = grad_sums[8] + jnp.sum(grad_middle * normed_first, 0)
        grad_sums[9] = grad_sums[9] + jnp.sum(grad_middle, 0)
        grad_first = normalize_back(grad_middle, normed_first, inverse_first, gain_first)
        grad_attn = grad_first.astype(jnp.bfloat16)
        grad_sums[6] = grad_sums[6] + jnp.sum(grad_attn.astype(jnp.float32), 0)
        grad_sums[3] = grad_sums[3] + jnp.einsum(
            "nc,nd->cd", mixed, grad_attn, preferred_element_type=jnp.float32
        )
        grad_mixed = head_split(
            jnp.einsum(
                "nd,cd->nc", grad_attn, output_full, preferred_element_type=jnp.float32
            ).astype(jnp.bfloat16)
        )
        attend_soft = jnp.exp(score_block(queries, keys_all) - log_total)
        grad_soft = jnp.einsum(
            "rshd,kshd->shrk", grad_mixed, values_all, preferred_element_type=jnp.float32
        )
        grad_values_all = jnp.einsum(
            "shrk,rshd->kshd",
            attend_soft.astype(jnp.bfloat16),
            grad_mixed,
            preferred_element_type=jnp.float32,
        )
        inner_prod = jnp.sum(grad_soft * attend_soft, -1, keepdims=True)
        grad_scores = (attend_soft * (grad_soft - inner_prod)).astype(jnp.bfloat16)
        grad_queries = (
            jnp.einsum("shrk,kshd->rshd", grad_scores, keys_all, preferred_element_type=jnp.float32)
            * scale_factor
        )
        grad_queries = grad_queries.astype(jnp.bfloat16).reshape(row_count, heads_here * HEAD)
        grad_keys_all = (
            jnp.einsum("shrk,rshd->kshd", grad_scores, queries, preferred_element_type=jnp.float32)
            * scale_factor
        )
        grad_keys, grad_values = (
            lax.psum_scatter(
                grad_keys_all.astype(jnp.bfloat16), "context", scatter_dimension=0, tiled=True
            ).astype(jnp.float32),
            lax.psum_scatter(
                grad_values_all.astype(jnp.bfloat16), "context", scatter_dimension=0, tiled=True
            ).astype(jnp.float32),
        )
        grad_keys = grad_keys.astype(jnp.bfloat16).reshape(row_count, heads_here * HEAD)
        grad_values = grad_values.astype(jnp.bfloat16).reshape(row_count, heads_here * HEAD)
        grad_sums[12] = grad_sums[12] + jnp.sum(grad_queries.astype(jnp.float32), 0)
        grad_sums[13] = grad_sums[13] + jnp.sum(grad_values.astype(jnp.float32), 0)
        grad_sums[0] = grad_sums[0] + jnp.einsum(
            "nd,nc->dc", flat_in, grad_queries, preferred_element_type=jnp.float32
        )
        grad_sums[1] = grad_sums[1] + jnp.einsum(
            "nd,nc->dc", flat_in, grad_keys, preferred_element_type=jnp.float32
        )
        grad_sums[2] = grad_sums[2] + jnp.einsum(
            "nd,nc->dc", flat_in, grad_values, preferred_element_type=jnp.float32
        )
        partial_value = jnp.einsum(
            "nc,dc->nd", grad_queries, query_full, preferred_element_type=jnp.float32
        )
        partial_value = partial_value + jnp.einsum(
            "nc,dc->nd", grad_keys, key_full, preferred_element_type=jnp.float32
        )
        partial_value = partial_value + jnp.einsum(
            "nc,dc->nd", grad_values, value_full, preferred_element_type=jnp.float32
        )
        return (grad_first + join_back(partial_value), grad_sums)

    current = stream.reshape(row_count, model_width).astype(jnp.float32)
    stored_all = []
    squares_all = []
    for repeat in range(LAYERS):
        weights = fetch_weights()
        (
            forward_query_full,
            forward_key_full,
            forward_value_full,
            forward_output_full,
            forward_inner_full,
            forward_outer_full,
            forward_bias_output,
            forward_bias_outer,
            forward_gain_first,
            forward_shift_first,
            forward_gain_second,
            forward_shift_second,
        ) = weights
        forward_flat_in = current.astype(jnp.bfloat16)
        forward_queries = head_split(
            (
                jnp.dot(forward_flat_in, forward_query_full, preferred_element_type=jnp.float32)
                + query_bias
            ).astype(jnp.bfloat16)
        )
        keys_here = head_split(
            jnp.dot(forward_flat_in, forward_key_full, preferred_element_type=jnp.float32).astype(
                jnp.bfloat16
            )
        )
        values_here = head_split(
            (
                jnp.dot(forward_flat_in, forward_value_full, preferred_element_type=jnp.float32)
                + value_bias
            ).astype(jnp.bfloat16)
        )
        forward_keys_all = lax.all_gather(keys_here, "context", axis=0, tiled=True)
        forward_values_all = lax.all_gather(values_here, "context", axis=0, tiled=True)
        scores = score_block(forward_queries, forward_keys_all)
        row_top = jnp.max(scores, -1, keepdims=True)
        exponent = jnp.exp(scores - row_top)
        row_total = jnp.sum(exponent, -1, keepdims=True)
        forward_attend_soft = (exponent / row_total).astype(jnp.bfloat16)
        forward_log_total = row_top + jnp.log(row_total)
        forward_mixed = jnp.einsum(
            "shrk,kshd->rshd",
            forward_attend_soft,
            forward_values_all,
            preferred_element_type=jnp.float32,
        )
        forward_mixed = forward_mixed.astype(jnp.bfloat16).reshape(row_count, heads_here * HEAD)
        attn_out = (
            join_partial(
                jnp.dot(forward_mixed, forward_output_full, preferred_element_type=jnp.float32)
            )
            + forward_bias_output
        )
        middle, forward_normed_first, forward_inverse_first = normalize(
            current + attn_out, forward_gain_first, forward_shift_first
        )
        forward_middle_low = middle.astype(jnp.bfloat16)
        forward_inner_pre = (
            jnp.dot(forward_middle_low, forward_inner_full, preferred_element_type=jnp.float32)
            + inner_bias
        )
        forward_inner_act = gelu_tanh(forward_inner_pre).astype(jnp.bfloat16)
        outer_out = (
            join_partial(
                jnp.dot(forward_inner_act, forward_outer_full, preferred_element_type=jnp.float32)
            )
            + forward_bias_outer
        )
        produced, forward_normed_second, forward_inverse_second = normalize(
            middle + outer_out, forward_gain_second, forward_shift_second
        )
        squares = jnp.stack(
            [
                jnp.sum(row_live * current * current),
                jnp.sum(row_live * attn_out * attn_out),
                jnp.sum(row_live * outer_out * outer_out),
            ]
        )
        forward_stored = (
            forward_flat_in,
            forward_queries,
            forward_keys_all,
            forward_values_all,
            forward_log_total,
            forward_mixed,
            forward_normed_first,
            forward_inverse_first,
            forward_middle_low,
            forward_inner_pre,
            forward_normed_second,
            forward_inverse_second,
        )
        current, stored, squares = (produced, forward_stored, squares)
        stored_all.append(stored)
        squares_all.append(squares)
    result = (current * row_live).astype(jnp.bfloat16).reshape(slot_count, seq_count, model_width)
    grad_next = cotangent.reshape(row_count, model_width).astype(jnp.float32) * row_live
    grad_sums = [jnp.zeros(member.shape, jnp.float32) for member in weights]
    grad_sums = grad_sums + [
        jnp.zeros(query_bias.shape, jnp.float32),
        jnp.zeros(value_bias.shape, jnp.float32),
        jnp.zeros(inner_bias.shape, jnp.float32),
    ]
    shared = [None] * 12
    for repeat in reversed(range(LAYERS)):
        weights = fetch_weights()
        backward_grad_sums = grad_sums
        (
            backward_query_full,
            backward_key_full,
            backward_value_full,
            backward_output_full,
            backward_inner_full,
            backward_outer_full,
            backward_bias_output,
            backward_bias_outer,
            backward_gain_first,
            backward_shift_first,
            backward_gain_second,
            backward_shift_second,
        ) = weights
        (
            backward_flat_in,
            backward_queries,
            backward_keys_all,
            backward_values_all,
            backward_log_total,
            backward_mixed,
            backward_normed_first,
            backward_inverse_first,
            backward_middle_low,
            backward_inner_pre,
            backward_normed_second,
            backward_inverse_second,
        ) = stored_all[repeat]
        backward_grad_sums = list(backward_grad_sums)
        backward_grad_sums[10] = backward_grad_sums[10] + jnp.sum(
            grad_next * backward_normed_second, 0
        )
        backward_grad_sums[11] = backward_grad_sums[11] + jnp.sum(grad_next, 0)
        grad_second = normalize_back(
            grad_next, backward_normed_second, backward_inverse_second, backward_gain_second
        )
        grad_outer = grad_second.astype(jnp.bfloat16)
        backward_grad_sums[7] = backward_grad_sums[7] + jnp.sum(grad_outer.astype(jnp.float32), 0)
        inner_act = gelu_tanh(backward_inner_pre).astype(jnp.bfloat16)
        backward_grad_sums[5] = backward_grad_sums[5] + jnp.einsum(
            "nf,nd->fd", inner_act, grad_outer, preferred_element_type=jnp.float32
        )
        grad_act = jnp.einsum(
            "nd,fd->nf", grad_outer, backward_outer_full, preferred_element_type=jnp.float32
        )
        unused_value, gelu_pull = jax.vjp(gelu_tanh, backward_inner_pre)
        grad_inner = gelu_pull(grad_act)[0].astype(jnp.bfloat16)
        backward_grad_sums[14] = backward_grad_sums[14] + jnp.sum(grad_inner.astype(jnp.float32), 0)
        backward_grad_sums[4] = backward_grad_sums[4] + jnp.einsum(
            "nd,nf->df", backward_middle_low, grad_inner, preferred_element_type=jnp.float32
        )
        backward_grad_middle = grad_second + join_back(
            jnp.einsum(
                "nf,df->nd", grad_inner, backward_inner_full, preferred_element_type=jnp.float32
            )
        )
        grad_middle = backward_grad_middle
        grad_sums = backward_grad_sums
        grad_next, grad_sums = backward_attn(grad_middle, stored_all[repeat], weights, grad_sums)
    shared = (
        lax.psum_scatter(grad_sums[0], ("fsdp", "context"), scatter_dimension=0, tiled=True),
        lax.psum_scatter(grad_sums[1], ("fsdp", "context"), scatter_dimension=0, tiled=True),
        lax.psum_scatter(grad_sums[2], ("fsdp", "context"), scatter_dimension=0, tiled=True),
        lax.psum_scatter(grad_sums[3], ("fsdp", "context"), scatter_dimension=1, tiled=True),
        lax.psum_scatter(grad_sums[4], ("fsdp", "context"), scatter_dimension=0, tiled=True),
        lax.psum_scatter(grad_sums[5], ("fsdp", "context"), scatter_dimension=1, tiled=True),
        lax.psum_scatter(grad_sums[6], ("fsdp", "context"), scatter_dimension=0, tiled=True),
        lax.psum_scatter(grad_sums[7], ("fsdp", "context"), scatter_dimension=0, tiled=True),
        lax.psum_scatter(grad_sums[8], ("fsdp", "context"), scatter_dimension=0, tiled=True),
        lax.psum_scatter(grad_sums[9], ("fsdp", "context"), scatter_dimension=0, tiled=True),
        lax.psum_scatter(grad_sums[10], ("fsdp", "context"), scatter_dimension=0, tiled=True),
        lax.psum_scatter(grad_sums[11], ("fsdp", "context"), scatter_dimension=0, tiled=True),
    )
    counted = jnp.sum(row_live)
    bias_query, bias_value, bias_inner, square_total, count_total = lax.psum(
        (grad_sums[12], grad_sums[13], grad_sums[14], jnp.stack(squares_all), counted),
        ("fsdp", "context"),
    )
    root_values = jnp.sqrt(square_total / (count_total * model_width) + 1e-06)
    stream_grad = grad_next.reshape(slot_count, seq_count, model_width)
    return (
        result,
        stream_grad,
        shared[0],
        bias_query,
        shared[1],
        shared[2],
        bias_value,
        shared[3],
        shared[6],
        shared[8],
        shared[9],
        shared[4],
        bias_inner,
        shared[5],
        shared[7],
        shared[10],
        shared[11],
        root_values,
    )


def solution(mesh):
    in_specs = (
        P("context", "fsdp", None),
        P("fsdp"),
        P(("fsdp", "context"), "tensor"),
        P("tensor"),
        P(("fsdp", "context"), "tensor"),
        P(("fsdp", "context"), "tensor"),
        P("tensor"),
        P("tensor", ("fsdp", "context")),
        P(("fsdp", "context")),
        P(("fsdp", "context")),
        P(("fsdp", "context")),
        P(("fsdp", "context"), "tensor"),
        P("tensor"),
        P("tensor", ("fsdp", "context")),
        P(("fsdp", "context")),
        P(("fsdp", "context")),
        P(("fsdp", "context")),
        P("context", "fsdp", None),
    )
    out_specs = (
        P("context", "fsdp", None),
        P("context", "fsdp", None),
        P(("fsdp", "context"), "tensor"),
        P("tensor"),
        P(("fsdp", "context"), "tensor"),
        P(("fsdp", "context"), "tensor"),
        P("tensor"),
        P("tensor", ("fsdp", "context")),
        P(("fsdp", "context")),
        P(("fsdp", "context")),
        P(("fsdp", "context")),
        P(("fsdp", "context"), "tensor"),
        P("tensor"),
        P("tensor", ("fsdp", "context")),
        P(("fsdp", "context")),
        P(("fsdp", "context")),
        P(("fsdp", "context")),
        P(),
    )
    return jax.shard_map(body, mesh=mesh, in_specs=in_specs, out_specs=out_specs, check_vma=False)
```

profile of v0, /device:TPU:0, one launch (start us, length us, event | category | flops | bytes accessed | tf_op | source)
XLA Modules:
  0.0 4842.8 jit_solution(4979228013967287753)
XLA Ops:
  10.7 329.0 %all-gather.17.cloned.1.call-done = bf16[1024,512]{1,0:T(8,128)(2,1)} async-done(((bf16[16,512]{1,0:T(8,128)(2,1)}), bf16[1024,512]{1,0:T(8,128)(2,1)}) %all-gather.17.cloned.1.call-update) | async-done | bytes 1048592 | tf_op jit(solution)/shard_map/all_gather | solution.py:69
  342.9 326.1 %all-gather.11.cloned.1.call-done = bf16[1024,512]{1,0:T(8,128)(2,1)} async-done(((bf16[16,512]{1,0:T(8,128)(2,1)}), bf16[1024,512]{1,0:T(8,128)(2,1)}) %all-gather.11.cloned.1.call-update) | async-done | bytes 1048592 | tf_op jit(solution)/shard_map/all_gather | solution.py:70
  672.8 325.4 %all-gather.15.cloned.1.call-done = bf16[1024,512]{1,0:T(8,128)(2,1)} async-done(((bf16[16,512]{1,0:T(8,128)(2,1)}), bf16[1024,512]{1,0:T(8,128)(2,1)}) %all-gather.15.cloned.1.call-update) | async-done | bytes 1048592 | tf_op jit(solution)/shard_map/all_gather | solution.py:68
  1000.7 45.0 all-gather.19.cloned.1.call-done
  1053.9 40.2 all-gather.13.cloned.1.call-done
  1094.2 6.3 fusion.44
  1101.3 323.1 %all-gather.21.cloned.1.call-done = bf16[512,1024]{0,1:T(8,128)(2,1)} async-done(((bf16[512,16]{0,1:T(8,128)(2,1)}), bf16[512,1024]{0,1:T(8,128)(2,1)}) %all-gather.21.cloned.1.call-update) | async-done | bytes 1048592 | tf_op jit(solution)/shard_map/all_gather | solution.py:71
  1431.2 348.1 %all-reduce.13 = (bf16[1024]{0:T(1024)(128)(2,1)S(1)}, bf16[1024]{0:T(1024)(128)(2,1)S(1)}, bf16[1024]{0:T(1024)(128)(2,1)S(1)}, bf16[1024]{0:T(1024)(128)(2,1)S...) all-reduce(bf16[1024]{0:T(1024)(128)(2,1)S(1)} %dynamic-update-slic, ...), channel_id=1, replica_groups=mesh['fsdp'=8,'context'=8,'tensor'=2] {'fsdp','context'}, use_global_device_ids=true, to_apply=%add.2 | all-reduce | flops 6144 | bytes 24576
  1782.0 7.7 all-gather.23.cloned.1.call-done
  1789.7 4.9 convolution_add_fusion.3
  1794.7 331.5 %all-gather.25.cloned.1.call-done = bf16[2048,1024]{0,1:T(8,128)(2,1)} async-done(((bf16[2048,16]{0,1:T(8,128)(2,1)}), bf16[2048,1024]{0,1:T(8,128)(2,1)}) %all-gather.25.cloned.1.call-update) | async-done | bytes 4194320 | tf_op jit(solution)/shard_map/all_gather | solution.py:73
  2126.2 5.1 convolution_convert_fusion.5
  2131.9 23.9 all-reduce.25.cloned.1.call-done
  2168.4 41.0 all-gather.29.cloned.1.call-done
  2217.7 40.2 all-gather.27.cloned.1.call-done
  2257.9 6.3 fusion.45
  2270.2 23.3 all-reduce.27.cloned.1.call-done
  2305.7 22.6 all-reduce.29.cloned.1.call-done
  2332.3 5.4 convert_reduce_fusion.1
  2341.1 25.6 all-reduce.31.cloned.1.call-done
  2373.1 7.1 multiply_reduce_fusion.1
  2380.2 4.7 multiply_convert_fusion.1
  2387.7 3.9 copy.108
  2391.7 6.9 fusion.26
  2398.5 3.9 copy.110
  2402.7 4.5 convert_reduce_fusion.9
  2412.6 23.1 reduce-scatter.31.cloned.1.call-done
  2441.7 37.8 reduce-scatter.33.cloned.1.call-done
  2487.7 23.0 all-reduce.33.cloned.1.call-done
  2515.1 5.4 convert_reduce_fusion
  2524.1 25.3 all-reduce.35.cloned.1.call-done
  2549.4 3.9 multiply_reduce_fusion.4
  2557.8 7.1 multiply_reduce_fusion
  2564.9 4.7 multiply_convert_fusion
  2572.2 3.9 copy.112
  2576.2 6.8 fusion.29
  2583.1 4.0 copy.114
  2587.3 4.5 convert_reduce_fusion.8
  2597.0 23.4 reduce-scatter.35.cloned.1.call-done
  2626.4 38.0 reduce-scatter.37.cloned.1.call-done
  2690.7 4.7 convolution_add_fusion.1
  2699.8 4.7 convolution_add_fusion
  2711.7 345.6 %all-reduce.12 = (f32[512]{0:T(512)}, f32[512]{0:T(512)}, f32[1024]{0:T(1024)S(1)}, f32[1024]{0:T(1024)S(1)}, f32[1024]{0:T(1024)S(1)}, /*index=5*/f32[2048]{0:T...) all-reduce(f32[512]{0:T(512)S(1)} %add.373, ...), channel_id=1, replica_groups=mesh['fsdp'=8,'context'=8,'tensor'=2] {'fsdp','context'}, use_global_device_ids=true, to_apply=%region_37.38 | all-reduce | flops 9223 | bytes 73784 | tf_op jit(solution)/shard_map/psum | solution.py:378
  3064.9 340.1 %reduce-scatter.25.cloned.1.call-done = f32[512,16]{0,1:T(8,128)} async-done(((f32[512,1024]{0,1:T(8,128)}), f32[512,16]{0,1:T(8,128)}) %reduce-scatter.25.cloned.1.call-update) | async-done | bytes 32784 | tf_op jit(solution)/shard_map/reduce_scatter | solution.py:367
  3405.0 350.6 %reduce-scatter.21.cloned.1.call-done = f32[16,512]{1,0:T(8,128)} async-done(((f32[1024,512]{1,0:T(8,128)}), f32[16,512]{1,0:T(8,128)}) %reduce-scatter.21.cloned.1.call-update) | async-done | bytes 32784 | tf_op jit(solution)/shard_map/reduce_scatter | solution.py:365
  3755.6 350.6 %reduce-scatter.23.cloned.1.call-done = f32[16,512]{1,0:T(8,128)} async-done(((f32[1024,512]{1,0:T(8,128)}), f32[16,512]{1,0:T(8,128)}) %reduce-scatter.23.cloned.1.call-update) | async-done | bytes 32784 | tf_op jit(solution)/shard_map/reduce_scatter | solution.py:366
  4106.2 364.2 %reduce-scatter.27.cloned.1.call-done = f32[16,2048]{1,0:T(8,128)} async-done(((f32[1024,2048]{1,0:T(8,128)}), f32[16,2048]{1,0:T(8,128)}) %reduce-scatter.27.cloned.1.call-update) | async-done | bytes 131088 | tf_op jit(solution)/shard_map/reduce_scatter | solution.py:368
  4470.4 365.3 %reduce-scatter.29.cloned.1.call-done = f32[2048,16]{0,1:T(8,128)} async-done(((f32[2048,1024]{0,1:T(8,128)}), f32[2048,16]{0,1:T(8,128)}) %reduce-scatter.29.cloned.1.call-update) | async-done | bytes 131088 | tf_op jit(solution)/shard_map/reduce_scatter | solution.py:369
  (381 shorter events, 176.2 us)
Async XLA Ops:
  7.2 332.6 %all-gather.17.cloned.1.call-start = ((), (), s32[]{:S(2)}) async-start(), calls=%async_computation.13 | async-start | bytes 1064960 | tf_op jit(solution)/shard_map/all_gather | solution.py:69
  7.9 661.1 %all-gather.11.cloned.1.call-start = ((), (), s32[]{:S(2)}) async-start(), calls=%async_computation.10 | async-start | bytes 1064960 | tf_op jit(solution)/shard_map/all_gather | solution.py:70
  8.7 989.6 %all-gather.15.cloned.1.call-start = ((), (), s32[]{:S(2)}) async-start(), calls=%async_computation.12 | async-start | bytes 1064960 | tf_op jit(solution)/shard_map/all_gather | solution.py:68
  9.4 1036.3 %all-gather.19.cloned.1.call-start = ((), (), s32[]{:S(2)}) async-start(), calls=%async_computation.14 | async-start | bytes 2359296 | tf_op jit(solution)/shard_map/all_gather | solution.py:229
  10.7 332.2 %copy-start.67 = (bf16[512]{0:T(512)(128)(2,1)S(1)}, bf16[512]{0:T(512)(128)(2,1)}, u32[]{:S(2)}) copy-start(bf16[512]{0:T(512)(128)(2,1)} %param.24) | copy-start | bytes 3076
  342.8 329.9 %copy-start.64 = (s32[2]{0:T(128)S(1)}, s32[2]{0:T(128)}, u32[]{:S(2)}) copy-start(s32[2]{0:T(128)} %param.19) | copy-start | bytes 28
  342.8 330.0 %copy-start.68 = (bf16[512]{0:T(512)(128)(2,1)S(1)}, bf16[512]{0:T(512)(128)(2,1)}, u32[]{:S(2)}) copy-start(bf16[512]{0:T(512)(128)(2,1)} %param.21) | copy-start | bytes 3076
  342.9 751.3 %all-gather.13.cloned.1.call-start = ((), (), s32[]{:S(2)}) async-start(), calls=%async_computation.11 | async-start | bytes 2359296 | tf_op jit(solution)/shard_map/all_gather | solution.py:230
  672.1 752.3 %all-gather.21.cloned.1.call-start = ((), (), s32[]{:S(2)}) async-start(), calls=%async_computation.15 | async-start | bytes 1064960 | tf_op jit(solution)/shard_map/all_gather | solution.py:71
  672.7 1106.6 %all-reduce.23.cloned.1.call-start = ((), (), s32[]{:S(2)}) async-start(), calls=%async_computation.16 | async-start | bytes 1048576 | tf_op jit(solution)/shard_map/psum | solution.py:83
  1000.7 48.0 copy-start.44
  1100.4 328.0 %copy-start.63 = (bf16[2048]{0:T(1024)(128)(2,1)S(1)}, bf16[2048]{0:T(1024)(128)(2,1)}, u32[]{:S(2)}) copy-start(bf16[2048]{0:T(1024)(128)(2,1)} %param.30) | copy-start | bytes 12292
  1100.4 328.1 %copy-start.66 = (u32[128]{0:T(128)S(1)}, u32[128]{0:T(128)}, u32[]{:S(2)}) copy-start(u32[128]{0:T(128)} %constant.67) | copy-start | bytes 1540
  1100.5 329.3 %copy-start.74 = (bf16[16]{0:T(256)(128)(2,1)S(1)}, bf16[16]{0:T(256)(128)(2,1)}, u32[]{:S(2)}) copy-start(bf16[16]{0:T(256)(128)(2,1)} %param.28) | copy-start | bytes 100
  1100.5 329.5 %copy-start.75 = (bf16[16]{0:T(256)(128)(2,1)S(1)}, bf16[16]{0:T(256)(128)(2,1)}, u32[]{:S(2)}) copy-start(bf16[16]{0:T(256)(128)(2,1)} %param.27) | copy-start | bytes 100
  1100.5 329.8 %copy-start.76 = (bf16[16]{0:T(256)(128)(2,1)S(1)}, bf16[16]{0:T(256)(128)(2,1)}, u32[]{:S(2)}) copy-start(bf16[16]{0:T(256)(128)(2,1)} %param.26) | copy-start | bytes 100
  1100.5 330.0 %copy-start.77 = (bf16[16]{0:T(256)(128)(2,1)S(1)}, bf16[16]{0:T(256)(128)(2,1)}, u32[]{:S(2)}) copy-start(bf16[16]{0:T(256)(128)(2,1)} %param.32) | copy-start | bytes 100
  1100.5 330.2 %copy-start.78 = (bf16[16]{0:T(256)(128)(2,1)S(1)}, bf16[16]{0:T(256)(128)(2,1)}, u32[]{:S(2)}) copy-start(bf16[16]{0:T(256)(128)(2,1)} %param.34) | copy-start | bytes 100
  1100.5 330.4 %copy-start.79 = (bf16[16]{0:T(256)(128)(2,1)S(1)}, bf16[16]{0:T(256)(128)(2,1)}, u32[]{:S(2)}) copy-start(bf16[16]{0:T(256)(128)(2,1)} %param.33) | copy-start | bytes 100
  1101.3 680.7 %copy-start.39 = (bf16[256,512]{1,0:T(8,128)(2,1)}, bf16[256,512]{1,0:T(8,128)(2,1)S(1)}, u32[]{:S(2)}) copy-start(bf16[256,512]{1,0:T(8,128)(2,1)S(1)} %reshape.282) | copy-start | bytes 786436
  1426.9 362.8 %all-gather.23.cloned.1.call-start = ((), (), s32[]{:S(2)}) async-start(), calls=%async_computation.17 | async-start | bytes 4259840 | tf_op jit(solution)/shard_map/all_gather | solution.py:72
  1427.6 698.5 %all-gather.25.cloned.1.call-start = ((), (), s32[]{:S(2)}) async-start(), calls=%async_computation.18 | async-start | bytes 4259840 | tf_op jit(solution)/shard_map/all_gather | solution.py:73
  1428.4 727.4 %all-reduce.25.cloned.1.call-start = ((), (), s32[]{:S(2)}) async-start(), calls=%async_computation.19 | async-start | bytes 1048576 | tf_op jit(solution)/shard_map/psum | solution.py:83
  1428.5 366.2 %copy-start.61 = (f32[2048]{0:T(1024)}, f32[2048]{0:T(1024)S(1)}, u32[]{:S(2)}) copy-start(f32[2048]{0:T(1024)S(1)} %convert_element_type.304) | copy-start | bytes 24580
  2131.3 78.1 %all-gather.29.cloned.1.call-start = ((), (), s32[]{:S(2)}) async-start(), calls=%async_computation.21 | async-start | bytes 2359296 | tf_op jit(solution)/shard_map/all_gather | solution.py:229
  2160.6 133.0 %copy-start.14 = (f32[256,1024]{1,0:T(8,128)}, f32[256,1024]{1,0:T(8,128)S(1)}, u32[]{:S(2)}) copy-start(f32[256,1024]{1,0:T(8,128)S(1)} %get-tuple-element.68) | copy-start | bytes 3145732
  2162.5 95.4 %all-gather.27.cloned.1.call-start = ((), (), s32[]{:S(2)}) async-start(), calls=%async_computation.20 | async-start | bytes 2359296 | tf_op jit(solution)/shard_map/all_gather | solution.py:230
  2165.7 127.9 %all-reduce.27.cloned.1.call-start = ((), (), s32[]{:S(2)}) async-start(), calls=%async_computation.22 | async-start | bytes 1048576 | tf_op jit(solution)/shard_map/psum | solution.py:83
  2168.4 44.0 copy-start.46
  2217.6 49.1 %copy-start.11 = (bf16[512,1024]{0,1:T(8,128)(2,1)S(1)}, bf16[512,1024]{0,1:T(8,128)(2,1)}, u32[]{:S(2)}) copy-start(bf16[512,1024]{0,1:T(8,128)(2,1)} %all-gather.21.cloned.1.call-done) | copy-start | bytes 3145732
  2268.0 60.3 %all-reduce.29.cloned.1.call-start = ((), (), s32[]{:S(2)}) async-start(), calls=%async_computation.23 | async-start | bytes 1048576 | tf_op jit(solution)/shard_map/psum | solution.py:83
  2302.5 64.1 %all-reduce.31.cloned.1.call-start = ((), (), s32[]{:S(2)}) async-start(), calls=%async_computation.24 | async-start | bytes 1048576 | tf_op jit(solution)/shard_map/psum | solution.py:86
  2332.3 34.3 copy-start.5
  2340.9 94.8 %reduce-scatter.31.cloned.1.call-start = ((), (), s32[]{:S(2)}) async-start(), calls=%async_computation.34 | async-start | bytes 2359296
  2391.6 88.0 %reduce-scatter.33.cloned.1.call-start = ((), (), s32[]{:S(2)}) async-start(), calls=%async_computation.35 | async-start | bytes 2359296
  2402.5 108.2 %all-reduce.33.cloned.1.call-start = ((), (), s32[]{:S(2)}) async-start(), calls=%async_computation.25 | async-start | bytes 1048576 | tf_op jit(solution)/shard_map/psum | solution.py:86
  2409.8 31.9 copy-start.35
  2487.6 61.8 %all-reduce.35.cloned.1.call-start = ((), (), s32[]{:S(2)}) async-start(), calls=%async_computation.26 | async-start | bytes 1048576 | tf_op jit(solution)/shard_map/psum | solution.py:86
  2523.6 96.7 %reduce-scatter.35.cloned.1.call-start = ((), (), s32[]{:S(2)}) async-start(), calls=%async_computation.36 | async-start | bytes 2359296
  2576.2 88.2 %reduce-scatter.37.cloned.1.call-start = ((), (), s32[]{:S(2)}) async-start(), calls=%async_computation.37 | async-start | bytes 2359296
  2587.0 475.0 %all-reduce.37.cloned.1.call-start = ((), (), s32[]{:S(2)}) async-start(), calls=%async_computation.27 | async-start | bytes 1048576 | tf_op jit(solution)/shard_map/psum | solution.py:86
  2673.9 391.0 %reduce-scatter.19.cloned.1.call-start = ((), (), s32[]{:S(2)}) async-start(), calls=%async_computation.28 | async-start | bytes 2129920 | tf_op jit(solution)/shard_map/reduce_scatter | solution.py:364
  2677.4 727.6 %reduce-scatter.25.cloned.1.call-start = ((), (), s32[]{:S(2)}) async-start(), calls=%async_computation.31 | async-start | bytes 2129920 | tf_op jit(solution)/shard_map/reduce_scatter | solution.py:367
  2681.4 1074.2 %reduce-scatter.21.cloned.1.call-start = ((), (), s32[]{:S(2)}) async-start(), calls=%async_computation.29 | async-start | bytes 2129920 | tf_op jit(solution)/shard_map/reduce_scatter | solution.py:365
  2684.8 1421.4 %reduce-scatter.23.cloned.1.call-start = ((), (), s32[]{:S(2)}) async-start(), calls=%async_computation.30 | async-start | bytes 2129920 | tf_op jit(solution)/shard_map/reduce_scatter | solution.py:366
  2688.1 1782.4 %reduce-scatter.27.cloned.1.call-start = ((), (), s32[]{:S(2)}) async-start(), calls=%async_computation.32 | async-start | bytes 8519680 | tf_op jit(solution)/shard_map/reduce_scatter | solution.py:368
  2695.4 2140.3 %reduce-scatter.29.cloned.1.call-start = ((), (), s32[]{:S(2)}) async-start(), calls=%async_computation.33 | async-start | bytes 8519680 | tf_op jit(solution)/shard_map/reduce_scatter | solution.py:369
  2704.6 357.5 %copy-start.18 = (f32[256,1024]{1,0:T(8,128)S(1)}, f32[256,1024]{1,0:T(8,128)}, u32[]{:S(2)}) copy-start(f32[256,1024]{1,0:T(8,128)} %copy-done.16) | copy-start | bytes 3145732
  (60 other events, 233.2 us)
Sparse Core Ops, SparseCore 0:
  9.7 330.0 all-gather.16
  341.4 327.5 all-gather.10
  670.7 327.5 all-gather.14
  1000.3 45.3 all-gather.18
  1047.7 46.4 all-gather.12
  1095.7 328.6 all-gather.20
  1427.4 24.2 all-reduce.22
  1453.4 336.2 all-gather.22
  1791.5 334.6 all-gather.24
  2131.4 24.3 all-reduce.24
  2162.6 46.7 all-gather.28
  2211.4 46.4 all-gather.26
  2268.1 25.3 all-reduce.26
  2302.7 25.6 all-reduce.28
  2341.0 25.6 all-reduce.30
  2391.7 43.9 reduce-scatter.30
  2438.1 41.4 reduce-scatter.32
  2487.8 22.9 all-reduce.32
  2523.7 25.6 all-reduce.34
  2576.3 44.0 reduce-scatter.34
  2622.9 41.4 reduce-scatter.36
  2674.0 22.7 all-reduce.36
  2699.8 354.6 reduce-scatter.18
  3057.3 347.6 reduce-scatter.24
  3407.9 347.6 reduce-scatter.20
  3758.5 347.6 reduce-scatter.22
  4109.0 361.3 reduce-scatter.26
  4473.4 362.3 reduce-scatter.28
where the time goes:
time: 4850 us; the launch traced here: 4840 us
  waiting for transfers between devices  3850 us (79%)
  blocking collectives  694 us (14%)
  matrix products  141 us (3%)
  local copies, waits for them, and re-layouts  89.6 us (2%)
    reduce_scatter x1, waiting for transfers between devices, body(): lax.psum_scatter(grad_sums[5], ('fsdp', 'context'), scatter_dimension=1,...  365 us
    reduce_scatter x1, waiting for transfers between devices, body(): lax.psum_scatter(grad_sums[4], ('fsdp', 'context'), scatter_dimension=0,...  364 us
    reduce_scatter x1, waiting for transfers between devices, body(): lax.psum_scatter(grad_sums[2], ('fsdp', 'context'), scatter_dimension=0,...  351 us
    reduce_scatter x1, waiting for transfers between devices, body(): lax.psum_scatter(grad_sums[1], ('fsdp', 'context'), scatter_dimension=0,...  351 us
    unnamed x1, blocking collectives  348 us
    psum x1, blocking collectives, body(): lax.psum((grad_sums[12], grad_sums[13], grad_sums[14], jnp.stack(squares_...  346 us
    reduce_scatter x1, waiting for transfers between devices, body(): lax.psum_scatter(grad_sums[3], ('fsdp', 'context'), scatter_dimension=1,...  340 us
    all_gather x1, waiting for transfers between devices, fetch_weights(): lax.all_gather(outer_weight, ('fsdp', 'context'), axis=1, tiled=True)  331 us
  transfers between devices with their start and end apart: 28, of which 25 were waited for; matrix products, arithmetic and copies ran while one was open for 3% of the time, Pallas kernels for 0%

commit v1 on v0

--- a/solution.py
+++ b/solution.py
@@ -1,12 +1,203 @@
+import functools
 import math
 
 import jax
 import jax.numpy as jnp
 from jax import lax
+from jax.experimental import pallas as pl
+from jax.experimental.pallas import tpu as pltpu
 from jax.sharding import PartitionSpec as P
 
 HEAD = 64
 LAYERS = 2
+MESH = pl.DeviceIdType.MESH
+LANES = 128
+
+
+def place():
+    f = lax.axis_index("fsdp"); c = lax.axis_index("context"); t = lax.axis_index("tensor")
+    return {"x": 2*(f//4)+c//4, "y": c%4, "z": f%4, "t": t}
+
+def device(at):
+    x = at["x"]
+    return ((x//2)*4+at["z"], (x%2)*4+at["y"], at["t"])
+
+def shifted(at, axis, step):
+    moved = dict(at); moved[axis] = lax.rem(at[axis]+step+4, 4)
+    return moved
+
+def greet(at, steps):
+    barrier = pltpu.get_barrier_semaphore()
+    for axis in "xyz":
+        for step in steps:
+            pl.semaphore_signal(barrier, inc=1, device_id=device(shifted(at,axis,step)), device_id_type=MESH)
+    pl.semaphore_wait(barrier, 3*len(steps))
+
+ORDERS = ("zyx","yxz","xzy")
+
+def view(ref, at, whole, cols):
+    x = at["x"]
+    xh = slice(None) if "x" in whole else x//2
+    xl = slice(None) if "x" in whole else x%2
+    z = slice(None) if "z" in whole else at["z"]
+    y = slice(None) if "y" in whole else at["y"]
+    return ref.at[xh, z, xl, y, :, pl.ds(cols[0], cols[1])]
+
+def parts_of(width):
+    tiles = width//LANES
+    cuts = [tiles*i//6*LANES for i in range(7)]
+    return [((cuts[2*i], cuts[2*i+1]-cuts[2*i]), (cuts[2*i+1], cuts[2*i+2]-cuts[2*i+1])) for i in range(3)]
+
+def gather_kernel(own_ref, all_ref, own_sem, send_sem, recv_sem):
+    at = place()
+    width = own_ref.shape[-1]
+    parts = parts_of(width)
+    x=at["x"]
+    mine = pltpu.make_async_copy(own_ref, all_ref.at[x//2, at["z"], x%2, at["y"]], own_sem)
+    mine.start()
+    greet(at, (1,-1))
+    mine.wait()
+
+    def send(part, phase, kind, whole, origin, cols, axis, step):
+        block = view(all_ref, origin, whole, cols)
+        return pltpu.make_async_remote_copy(src_ref=block, dst_ref=block, send_sem=send_sem.at[part,phase,kind], recv_sem=recv_sem.at[part,phase,kind], device_id=device(shifted(at,axis,step)), device_id_type=MESH)
+
+    for phase in range(3):
+        first=[]; second=[]
+        for part,(order) in enumerate(ORDERS):
+            axis=order[phase]; whole=order[:phase]
+            lo,hi=parts[part]; both=(lo[0],lo[1]+hi[1])
+            r=send(part,phase,0,whole,at,both,axis,1); l=send(part,phase,1,whole,at,both,axis,-1)
+            r.start(); l.start(); first.append((r,l))
+        for part,(order) in enumerate(ORDERS):
+            axis=order[phase]; whole=order[:phase]
+            lo,hi=parts[part]
+            r,l=first[part]
+            r.wait_recv()
+            fr=send(part,phase,2,whole,shifted(at,axis,-1),lo,axis,1); fr.start()
+            l.wait_recv()
+            fl=send(part,phase,3,whole,shifted(at,axis,1),hi,axis,-1); fl.start()
+            second.append((fr,fl))
+        for part in range(3):
+            for c in second[part]: c.wait_recv()
+        for part in range(3):
+            for c in first[part]+second[part]: c.wait_send()
+
+def gather_all(own):
+    rows,width=own.shape
+    out=pl.pallas_call(gather_kernel,
+        out_shape=jax.ShapeDtypeStruct((2,4,2,4,rows,width), own.dtype),
+        in_specs=[pl.BlockSpec(memory_space=pl.ANY)], out_specs=pl.BlockSpec(memory_space=pl.ANY),
+        scratch_shapes=[pltpu.SemaphoreType.DMA, pltpu.SemaphoreType.DMA((3,3,4)), pltpu.SemaphoreType.DMA((3,3,4))],
+        compiler_params=pltpu.CompilerParams(collective_id=1, has_side_effects=True),
+        name="gather_weights")(own)
+    return out
+
+def scatter_kernel(all_ref, small_ref, own_ref, total_ref, work, small_land, load_sem, send_sem, recv_sem, small_send, small_recv, *landings):
+    at = place()
+    parts = parts_of(all_ref.shape[-1])
+    loads=[]
+    for part in range(3):
+        lo,hi=parts[part]; both=pl.ds(lo[0],lo[1]+hi[1])
+        cp=pltpu.make_async_copy(all_ref.at[:,:,:,:,:,both], work.at[:,:,:,:,:,both], load_sem.at[part]); cp.start(); loads.append(cp)
+    greet(at, (1,2,3))
+    for cp in loads: cp.wait()
+
+    def push(part,phase,kind,origin,whole,cols,axis,step):
+        land=landings[phase*3+part]
+        src=view(work,origin,whole,cols)
+        return pltpu.make_async_remote_copy(src_ref=src,dst_ref=land.at[kind] if cols[1]==land.shape[-1] else land.at[kind,...,pl.ds(0,cols[1])],send_sem=send_sem.at[part,phase,kind],recv_sem=recv_sem.at[part,phase,kind],device_id=device(shifted(at,axis,step)),device_id_type=MESH)
+
+    def add(origin,whole,cols,land_list):
+        x=origin["x"]
+        xs=[(a,b) for a in range(2) for b in range(2)] if "x" in whole else [(x//2,x%2)]
+        zs=list(range(4)) if "z" in whole else [origin["z"]]
+        ys=list(range(4)) if "y" in whole else [origin["y"]]
+        sx="x" in whole; sz="z" in whole; sy="y" in whole
+        def one(ix,iz,iy):
+            xh,xl=(ix//2,ix%2) if sx else (x//2,x%2)
+            z=iz if sz else origin["z"]; y=iy if sy else origin["y"]
+            index=(xh,z,xl,y,slice(None),pl.ds(cols[0],cols[1]))
+            total=work[index].astype(jnp.float32)
+            for land,kind in land_list:
+                li=(kind,)
+                if sx: li+=(xh,)
+                if sz: li+=(z,)
+                if sx: li+=(xl,)
+                if sy: li+=(y,)
+                li+=(slice(None),pl.ds(0,cols[1]))
+                total=total+land[li].astype(jnp.float32)
+            work[index]=total.astype(work.dtype)
+        nx=4 if sx else 1; nz=4 if sz else 1; ny=4 if sy else 1
+        n=nx*nz*ny
+        def body(i,_):
+            one(i//(nz*ny), (i//ny)%nz, i%ny); return 0
+        if n==1: one(0,0,0)
+        else: lax.fori_loop(0,n,body,0)
+
+    total_ref[...]=small_ref[...]
+    for phase in range(3):
+        early=[]
+        small=[]
+        for step in (1,2,3):
+            cp=pltpu.make_async_remote_copy(src_ref=total_ref,dst_ref=small_land.at[phase,step-1],send_sem=small_send.at[phase,step-1],recv_sem=small_recv.at[phase,step-1],device_id=device(shifted(at,"xyz"[phase],step)),device_id_type=MESH)
+            cp.start(); small.append(cp)
+        for part in range(3):
+            order=ORDERS[part][::-1]; axis=order[phase]; whole=order[phase+1:]
+            lo,hi=parts[part]
+            far=shifted(at,axis,2); up=shifted(at,axis,1); down=shifted(at,axis,-1)
+            a=push(part,phase,0,far,whole,lo,axis,1); a.start()
+            b=push(part,phase,1,far,whole,hi,axis,-1); b.start()
+            c=push(part,phase,2,up,whole,hi,axis,1); c.start()
+            d=push(part,phase,3,down,whole,lo,axis,-1); d.start()
+            early.append((a,b,c,d))
+        late=[]
+        for part in range(3):
+            order=ORDERS[part][::-1]; axis=order[phase]; whole=order[phase+1:]
+            lo,hi=parts[part]; land=landings[phase*3+part]
+            up=shifted(at,axis,1); down=shifted(at,axis,-1)
+            a,b,c,d=early[part]
+            a.wait_recv(); add(up,whole,lo,[(land,0)])
+            e=push(part,phase,4,up,whole,lo,axis,1); e.start()
+            b.wait_recv(); add(down,whole,hi,[(land,1)])
+            f=push(part,phase,5,down,whole,hi,axis,-1); f.start()
+            late.append((e,f))
+        for part in range(3):
+            order=ORDERS[part][::-1]; axis=order[phase]; whole=order[phase+1:]
+            lo,hi=parts[part]; land=landings[phase*3+part]
+            a,b,c,d=early[part]; e,f=late[part]
+            c.wait_recv(); f.wait_recv()
+            add(at,whole,hi,[(land,2),(land,5)])
+            d.wait_recv(); e.wait_recv()
+            add(at,whole,lo,[(land,3),(land,4)])
+        for part in range(3):
+            for cp in early[part]+late[part]: cp.wait_send()
+        for cp in small: cp.wait_recv()
+        for cp in small: cp.wait_send()
+        total_ref[...]=total_ref[...]+small_land[phase,0]+small_land[phase,1]+small_land[phase,2]
+    x=at["x"]
+    own_ref[...]=work[x//2,at["z"],x%2,at["y"]].astype(jnp.float32)
+
+def scatter_all(whole, small):
+    rows,width=whole.shape[-2:]
+    parts=parts_of(width)
+    landings=[]
+    for phase in range(3):
+        for part in range(3):
+            order=ORDERS[part][::-1]; w=order[phase+1:]
+            shape=[6]
+            if "x" in w: shape.append(2)
+            if "z" in w: shape.append(4)
+            if "x" in w: shape.append(2)
+            if "y" in w: shape.append(4)
+            shape+= [rows, max(parts[part][0][1],parts[part][1][1])]
+            landings.append(pltpu.VMEM(tuple(shape), whole.dtype))
+    return pl.pallas_call(scatter_kernel,
+        out_shape=(jax.ShapeDtypeStruct((rows,width), jnp.float32),jax.ShapeDtypeStruct(small.shape, jnp.float32)),
+        in_specs=[pl.BlockSpec(memory_space=pl.ANY),pl.BlockSpec(memory_space=pltpu.VMEM)], out_specs=(pl.BlockSpec(memory_space=pltpu.VMEM),pl.BlockSpec(memory_space=pltpu.VMEM)),
+        scratch_shapes=[pltpu.VMEM(whole.shape, whole.dtype), pltpu.VMEM((3,3)+small.shape,jnp.float32), pltpu.SemaphoreType.DMA((3,)), pltpu.SemaphoreType.DMA((3,3,6)), pltpu.SemaphoreType.DMA((3,3,6)), pltpu.SemaphoreType.DMA((3,3)), pltpu.SemaphoreType.DMA((3,3))]+landings,
+        compiler_params=pltpu.CompilerParams(collective_id=2, has_side_effects=True, vmem_limit_bytes=60*2**20),
+        name="scatter_grads")(whole, small)
 
 
 def gelu_tanh(argument):
@@ -63,20 +254,38 @@
     position = lax.axis_index("context") * slot_count + jnp.arange(slot_count, dtype=jnp.int32)
     row_live = (position[:, None] < lengths[None, :]).astype(jnp.float32).reshape(row_count, 1)
 
+    extras = jnp.stack(
+        [output_bias, outer_bias, first_gain, first_shift, second_gain, second_shift], 1
+    )
+    packed = jnp.concatenate(
+        [
+            query_weight,
+            key_weight,
+            value_weight,
+            output_weight.T,
+            inner_weight,
+            outer_weight.T,
+            jnp.pad(extras, ((0, 0), (0, LANES - 6))),
+        ],
+        1,
+    )
+    gathered = gather_all(packed).reshape(model_width, packed.shape[1])
+    vectors = gathered[:, 6144:6150].T
+
     def fetch_weights():
         return (
-            lax.all_gather(query_weight, ("fsdp", "context"), axis=0, tiled=True),
-            lax.all_gather(key_weight, ("fsdp", "context"), axis=0, tiled=True),
-            lax.all_gather(value_weight, ("fsdp", "context"), axis=0, tiled=True),
-            lax.all_gather(output_weight, ("fsdp", "context"), axis=1, tiled=True),
-            lax.all_gather(inner_weight, ("fsdp", "context"), axis=0, tiled=True),
-            lax.all_gather(outer_weight, ("fsdp", "context"), axis=1, tiled=True),
-            lax.all_gather(output_bias, ("fsdp", "context"), axis=0, tiled=True),
-            lax.all_gather(outer_bias, ("fsdp", "context"), axis=0, tiled=True),
-            lax.all_gather(first_gain, ("fsdp", "context"), axis=0, tiled=True),
-            lax.all_gather(first_shift, ("fsdp", "context"), axis=0, tiled=True),
-            lax.all_gather(second_gain, ("fsdp", "context"), axis=0, tiled=True),
-            lax.all_gather(second_shift, ("fsdp", "context"), axis=0, tiled=True),
+            gathered[:, 0:512],
+            gathered[:, 512:1024],
+            gathered[:, 1024:1536],
+            gathered[:, 1536:2048].T,
+            gathered[:, 2048:4096],
+            gathered[:, 4096:6144].T,
+            vectors[0],
+            vectors[1],
+            vectors[2],
+            vectors[3],
+            vectors[4],
+            vectors[5],
         )
 
     def join_partial(partial_value):
@@ -360,25 +569,42 @@
         grad_middle = backward_grad_middle
         grad_sums = backward_grad_sums
         grad_next, grad_sums = backward_attn(grad_middle, stored_all[repeat], weights, grad_sums)
+    grad_extras = jnp.stack(grad_sums[6:12], 1)
+    grads = jnp.concatenate(
+        [
+            grad_sums[0],
+            grad_sums[1],
+            grad_sums[2],
+            grad_sums[3].T,
+            grad_sums[4],
+            grad_sums[5].T,
+            jnp.pad(grad_extras, ((0, 0), (0, LANES - 6))),
+        ],
+        1,
+    ).astype(jnp.bfloat16)
+    counted = jnp.sum(row_live)
+    small = jnp.concatenate(
+        [
+            grad_sums[12],
+            grad_sums[13],
+            grad_sums[14],
+            jnp.stack(squares_all).reshape(-1),
+            counted[None],
+            jnp.zeros((1024 - 7,), jnp.float32),
+        ]
+    ).reshape(32, LANES)
+    summed, total = scatter_all(grads.reshape(2, 4, 2, 4, 16, grads.shape[1]), small)
+    total = total.reshape(-1)
+    bias_query, bias_value, bias_inner = total[0:512], total[512:1024], total[1024:3072]
+    square_total, count_total = total[3072:3078].reshape(LAYERS, 3), total[3078]
     shared = (
-        lax.psum_scatter(grad_sums[0], ("fsdp", "context"), scatter_dimension=0, tiled=True),
-        lax.psum_scatter(grad_sums[1], ("fsdp", "context"), scatter_dimension=0, tiled=True),
-        lax.psum_scatter(grad_sums[2], ("fsdp", "context"), scatter_dimension=0, tiled=True),
-        lax.psum_scatter(grad_sums[3], ("fsdp", "context"), scatter_dimension=1, tiled=True),
-        lax.psum_scatter(grad_sums[4], ("fsdp", "context"), scatter_dimension=0, tiled=True),
-        lax.psum_scatter(grad_sums[5], ("fsdp", "context"), scatter_dimension=1, tiled=True),
-        lax.psum_scatter(grad_sums[6], ("fsdp", "context"), scatter_dimension=0, tiled=True),
-        lax.psum_scatter(grad_sums[7], ("fsdp", "context"), scatter_dimension=0, tiled=True),
-        lax.psum_scatter(grad_sums[8], ("fsdp", "context"), scatter_dimension=0, tiled=True),
-        lax.psum_scatter(grad_sums[9], ("fsdp", "context"), scatter_dimension=0, tiled=True),
-        lax.psum_scatter(grad_sums[10], ("fsdp", "context"), scatter_dimension=0, tiled=True),
-        lax.psum_scatter(grad_sums[11], ("fsdp", "context"), scatter_dimension=0, tiled=True),
-    )
-    counted = jnp.sum(row_live)
-    bias_query, bias_value, bias_inner, square_total, count_total = lax.psum(
-        (grad_sums[12], grad_sums[13], grad_sums[14], jnp.stack(squares_all), counted),
-        ("fsdp", "context"),
-    )
+        summed[:, 0:512],
+        summed[:, 512:1024],
+        summed[:, 1024:1536],
+        summed[:, 1536:2048].T,
+        summed[:, 2048:4096],
+        summed[:, 4096:6144].T,
+    ) + tuple(summed[:, 6144 + place_at] for place_at in range(6))
     root_values = jnp.sqrt(square_total / (count_total * model_width) + 1e-06)
     stream_grad = grad_next.reshape(slot_count, seq_count, model_width)
     return (

time: 4850 us -> 905 us (0.19)
  waiting for transfers between devices: 3850 us -> 434 us
  blocking collectives: 694 us -> 0 us
  Pallas kernels: 0 us -> 132 us
    reduce_scatter x6 -> x0, waiting for transfers between devices: 1770 us -> none  [the longest x1 365 us: body(): lax.psum_scatter(grad_sums[5], ('fsdp', 'context'), scatter_dimension=1,...]
    all_gather x6 -> x0, waiting for transfers between devices: 1640 us -> none  [the longest x1 331 us: fetch_weights(): lax.all_gather(outer_weight, ('fsdp', 'context'), axis=1, tiled=True)]
    unnamed x1 -> x0, blocking collectives: 348 us -> none
    psum x1 -> x0, blocking collectives: 346 us -> none  [body(): lax.psum((grad_sums[12], grad_sums[13], grad_sums[14], jnp.stack(squares_...]
    pallas_call x0 -> x2, Pallas kernels: none -> 132 us  [the longest x1 68.1 us: gather_all(): pl.pallas_call(gather_kernel, out_shape=jax.ShapeDtypeStruct((2, 4, 2, 4,...]
    unnamed x32 -> x20, waiting for transfers between devices: 127 us -> 87.6 us
  transfers between devices with their start and end apart: 28 -> 16, of which waited for: 25 -> 15; matrix products, arithmetic and copies ran while one was open for 3% -> 13% of each run, Pallas kernels for 0% -> 0%
where the time goes in v1:
time: 905 us; the launch traced here: 893 us
  waiting for transfers between devices  434 us (48%)
  matrix products  156 us (17%)
  Pallas kernels  132 us (15%)
  local copies, waits for them, and re-layouts  104 us (11%)
  other arithmetic  48.9 us (5%)
  between operations  16.1 us (2%)
    psum x4, waiting for transfers between devices, join_partial(): lax.psum(partial_value.astype(jnp.bfloat16), 'tensor').astype(jnp.float32)  95.4 us
    psum x4, waiting for transfers between devices, join_back(): lax.psum(partial_value.astype(jnp.bfloat16), 'tensor').astype(jnp.float32)  91.3 us
    unnamed x20, waiting for transfers between devices  87.6 us
    all_gather x2, waiting for transfers between devices, body(): lax.all_gather(values_here, 'context', axis=0, tiled=True)  80.4 us
    all_gather x2, waiting for transfers between devices, body(): forward_keys_all = lax.all_gather(keys_here, 'context', axis=0, tiled=True)  79.1 us
    pallas_call x1, Pallas kernels, gather_all(): pl.pallas_call(gather_kernel, out_shape=jax.ShapeDtypeStruct((2, 4, 2, 4,...  68.1 us
    pallas_call x1, Pallas kernels, scatter_all(): pl.pallas_call(scatter_kernel, out_shape=(jax.ShapeDtypeStruct((rows, wid...  63.5 us
    unnamed x156, local copies, waits for them, and re-layouts  53.8 us
  transfers between devices with their start and end apart: 16, of which 15 were waited for; matrix products, arithmetic and copies ran while one was open for 13% of the time, Pallas kernels for 0%

profile of v1, /device:TPU:0, one launch (start us, length us, event | category | flops | bytes accessed | tf_op | source)
XLA Modules:
  0.0 893.0 jit_solution(15508374664627227721)
XLA Ops:
  17.1 68.1 %gather_weights.1 = bf16[2,4,2,4,16,6272]{5,4,3,2,1,0:T(8,128)(2,1)} custom-call(bf16[16,6272]{1,0:T(8,128)(2,1)} %copy-done.51), custom_call_target="tpu_custom_call" | custom-call | tf_op jit(solution)/shard_map/gather_weights/pallas_call | solution.py:88
  95.0 38.1 %all-gather.7.cloned.1.call-done = bf16[1024,2,8,64]{0,3,2,1:T(8,128)(2,1)} async-done(((bf16[128,2,8,64]{0,3,2,1:T(8,128)(2,1)}), bf16[1024,2,8,64]{0,3,2,1:T(8,128)(2,1)}) %all-gather.7.cloned.1.call-update) | async-done | bytes 2097168 | tf_op jit(solution)/shard_map/all_gather | solution.py:438
  133.1 3.0 fusion.12
  136.1 3.2 copy-done
  141.3 40.2 %all-gather.5.cloned.1.call-done = bf16[1024,2,8,64]{0,3,2,1:T(8,128)(2,1)} async-done(((bf16[128,2,8,64]{0,3,2,1:T(8,128)(2,1)}), bf16[1024,2,8,64]{0,3,2,1:T(8,128)(2,1)}) %all-gather.5.cloned.1.call-update) | async-done | bytes 2097168 | tf_op jit(solution)/shard_map/all_gather | solution.py:439
  181.5 6.3 fusion.85
  192.6 24.1 %all-reduce.11.cloned.1.call-done = bf16[256,1024]{1,0:T(8,128)(2,1)} async-done(((bf16[256,1024]{1,0:T(8,128)(2,1)}), bf16[256,1024]{1,0:T(8,128)(2,1)}) %all-reduce.11.cloned.1.call-update) | async-done | bytes 524304 | tf_op jit(solution)/shard_map/psum | solution.py:292
  219.4 3.7 fusion.30
  224.5 4.5 fusion.69
  229.3 25.5 %all-reduce.13.cloned.1.call-done = bf16[256,1024]{1,0:T(8,128)(2,1)} async-done(((bf16[256,1024]{1,0:T(8,128)(2,1)}), bf16[256,1024]{1,0:T(8,128)(2,1)}) %all-reduce.13.cloned.1.call-update) | async-done | bytes 524304 | tf_op jit(solution)/shard_map/psum | solution.py:292
  270.4 41.0 %all-gather.11.cloned.1.call-done = bf16[1024,2,8,64]{0,3,2,1:T(8,128)(2,1)} async-done(((bf16[128,2,8,64]{0,3,2,1:T(8,128)(2,1)}), bf16[1024,2,8,64]{0,3,2,1:T(8,128)(2,1)}) %all-gather.11.cloned.1.call-update) | async-done | bytes 2097168 | tf_op jit(solution)/shard_map/all_gather | solution.py:438
  311.3 3.0 fusion.13
  314.3 3.3 copy-done.1
  319.6 40.2 %all-gather.9.cloned.1.call-done = bf16[1024,2,8,64]{0,3,2,1:T(8,128)(2,1)} async-done(((bf16[128,2,8,64]{0,3,2,1:T(8,128)(2,1)}), bf16[1024,2,8,64]{0,3,2,1:T(8,128)(2,1)}) %all-gather.9.cloned.1.call-update) | async-done | bytes 2097168 | tf_op jit(solution)/shard_map/all_gather | solution.py:439
  359.8 6.3 fusion.86
  370.7 24.4 %all-reduce.15.cloned.1.call-done = bf16[256,1024]{1,0:T(8,128)(2,1)} async-done(((bf16[256,1024]{1,0:T(8,128)(2,1)}), bf16[256,1024]{1,0:T(8,128)(2,1)}) %all-reduce.15.cloned.1.call-update) | async-done | bytes 524304 | tf_op jit(solution)/shard_map/psum | solution.py:292
  396.6 3.5 fusion.33
  401.5 4.4 fusion.72
  406.5 3.7 multiply_reduce_fusion.18
  410.3 21.5 %all-reduce.17.cloned.1.call-done = bf16[256,1024]{1,0:T(8,128)(2,1)} async-done(((bf16[256,1024]{1,0:T(8,128)(2,1)}), bf16[256,1024]{1,0:T(8,128)(2,1)}) %all-reduce.17.cloned.1.call-update) | async-done | bytes 524304 | tf_op jit(solution)/shard_map/psum | solution.py:292
  435.5 5.4 convert_reduce_fusion.1
  441.9 4.4 fusion.63
  446.5 25.6 %all-reduce.19.cloned.1.call-done = bf16[256,1024]{1,0:T(8,128)(2,1)} async-done(((bf16[256,1024]{1,0:T(8,128)(2,1)}), bf16[256,1024]{1,0:T(8,128)(2,1)}) %all-reduce.19.cloned.1.call-update) | async-done | bytes 524304 | tf_op jit(solution)/shard_map/psum | solution.py:295
  479.6 7.1 multiply_reduce_fusion.1
  486.8 4.7 multiply_convert_fusion.1
  495.5 3.9 copy.136
  499.5 6.9 fusion.51
  506.4 3.9 copy.138
  510.6 4.5 convert_reduce_fusion.9
  520.5 23.2 %reduce-scatter.13.cloned.1.call-done = bf16[128,1024]{1,0:T(8,128)(2,1)} async-done(((bf16[1024,1024]{1,0:T(8,128)(2,1)}), bf16[128,1024]{1,0:T(8,128)(2,1)}) %reduce-scatter.13.cloned.1.call-update) | async-done | bytes 262160
  549.6 38.0 %reduce-scatter.15.cloned.1.call-done = bf16[128,1024]{1,0:T(8,128)(2,1)} async-done(((bf16[1024,1024]{1,0:T(8,128)(2,1)}), bf16[128,1024]{1,0:T(8,128)(2,1)}) %reduce-scatter.15.cloned.1.call-update) | async-done | bytes 262160
  596.9 23.1 %all-reduce.21.cloned.1.call-done = bf16[256,1024]{1,0:T(8,128)(2,1)} async-done(((bf16[256,1024]{1,0:T(8,128)(2,1)}), bf16[256,1024]{1,0:T(8,128)(2,1)}) %all-reduce.21.cloned.1.call-update) | async-done | bytes 524304 | tf_op jit(solution)/shard_map/psum | solution.py:295
  624.4 5.4 convert_reduce_fusion
  630.8 4.4 fusion.66
  635.6 25.3 %all-reduce.23.cloned.1.call-done = bf16[256,1024]{1,0:T(8,128)(2,1)} async-done(((bf16[256,1024]{1,0:T(8,128)(2,1)}), bf16[256,1024]{1,0:T(8,128)(2,1)}) %all-reduce.23.cloned.1.call-update) | async-done | bytes 524304 | tf_op jit(solution)/shard_map/psum | solution.py:295
  661.0 4.0 multiply_reduce_fusion.4
  671.7 6.8 fusion.54
  678.6 4.0 copy.142
  685.4 6.1 fusion.149
  691.4 4.8 fusion.135
  701.7 3.2 multiply_reduce_fusion
  711.1 4.1 copy.140
  717.4 7.0 add_convert_fusion.1
  724.5 3.4 add_convert_fusion
  731.4 4.0 maximum_bitcast_fusion
  744.7 26.1 %reduce-scatter.17.cloned.1.call-done = bf16[128,1024]{1,0:T(8,128)(2,1)} async-done(((bf16[1024,1024]{1,0:T(8,128)(2,1)}), bf16[128,1024]{1,0:T(8,128)(2,1)}) %reduce-scatter.17.cloned.1.call-update) | async-done | bytes 262160
  790.3 63.5 %scatter_grads.1 = (f32[16,6272]{1,0:T(8,128)}, f32[32,128]{1,0:T(8,128)}) custom-call(bf16[2,4,2,4,16,6272]{5,4,3,2,1,0:T(8,128)(2,1)} %constant_dynamic-update-slice_fusion.6.all_ref, f32[32,128]{1,0:T(8,128)} %bitcast.256), custom_call_target="tpu_custom_call" | custom-call | tf_op jit(solution)/shard_map/scatter_grads/pallas_call | solution.py:195
  866.1 17.3 %all-reduce.25.cloned.1.call-done = bf16[256,1024]{1,0:T(8,128)(2,1)} async-done(((bf16[256,1024]{1,0:T(8,128)(2,1)}), bf16[256,1024]{1,0:T(8,128)(2,1)}) %all-reduce.25.cloned.1.call-update) | async-done | bytes 524304 | tf_op jit(solution)/shard_map/psum | solution.py:295
  (339 shorter events, 169.0 us)
Async XLA Ops:
  7.2 125.9 %all-gather.7.cloned.1.call-start = ((), (), s32[]{:S(2)}) async-start(), calls=%async_computation.5 | async-start | bytes 2359296 | tf_op jit(solution)/shard_map/all_gather | solution.py:438
  17.1 68.2 %copy-start.36 = (bf16[128,2,1024]{2,1,0:T(2,128)(2,1)S(1)}, bf16[128,2,1024]{2,1,0:T(2,128)(2,1)}, u32[]{:S(2)}) copy-start(bf16[128,2,1024]{2,1,0:T(2,128)(2,1)} %param.18) | copy-start | bytes 1572868
  88.8 92.8 %all-gather.5.cloned.1.call-start = ((), (), s32[]{:S(2)}) async-start(), calls=%async_computation.4 | async-start | bytes 2359296 | tf_op jit(solution)/shard_map/all_gather | solution.py:439
  92.2 124.5 %all-reduce.11.cloned.1.call-start = ((), (), s32[]{:S(2)}) async-start(), calls=%async_computation.6 | async-start | bytes 1048576 | tf_op jit(solution)/shard_map/psum | solution.py:292
  94.9 41.2 %copy-start.30 = (bf16[128,2,8,64]{0,3,2,1:T(8,128)(2,1)}, bf16[128,2,8,64]{0,3,2,1:T(8,128)(2,1)S(1)}, u32[]{:S(2)}) copy-start(bf16[128,2,8,64]{0,3,2,1:T(8,128)(2,1)S(1)} %copy.102) | copy-start | bytes 786436
  188.6 34.6 %copy-start.44 = (bf16[256,512]{1,0:T(8,128)(2,1)}, bf16[256,512]{1,0:T(8,128)(2,1)S(1)}, u32[]{:S(2)}) copy-start(bf16[256,512]{1,0:T(8,128)(2,1)S(1)} %reshape.394) | copy-start | bytes 786436
  191.2 63.6 %all-reduce.13.cloned.1.call-start = ((), (), s32[]{:S(2)}) async-start(), calls=%async_computation.7 | async-start | bytes 1048576 | tf_op jit(solution)/shard_map/psum | solution.py:292
  192.6 30.6 %copy-start.55 = (f32[2048]{0:T(1024)}, f32[2048]{0:T(1024)S(1)}, u32[]{:S(2)}) copy-start(f32[2048]{0:T(1024)S(1)} %convert_element_type.313) | copy-start | bytes 24580
  224.5 30.3 %copy-start.5 = (bf16[256,1024]{1,0:T(8,128)(2,1)S(1)}, bf16[256,1024]{1,0:T(8,128)(2,1)}, u32[]{:S(2)}) copy-start(bf16[256,1024]{1,0:T(8,128)(2,1)} %all-reduce.11.cloned.1.call-done) | copy-start | bytes 1572868
  229.0 82.3 %all-gather.11.cloned.1.call-start = ((), (), s32[]{:S(2)}) async-start(), calls=%async_computation.9 | async-start | bytes 2359296 | tf_op jit(solution)/shard_map/all_gather | solution.py:438
  229.1 25.7 %copy-start.61 = (s32[128]{0:T(128)}, s32[128]{0:T(128)S(1)}, u32[]{:S(2)}) copy-start(s32[128]{0:T(128)S(1)} %iota_add_fusion) | copy-start | bytes 1540
  258.9 7.3 copy-start.53
  260.7 7.2 copy-start.20
  260.8 134.3 %copy-start.12 = (f32[256,1024]{1,0:T(8,128)}, f32[256,1024]{1,0:T(8,128)S(1)}, u32[]{:S(2)}) copy-start(f32[256,1024]{1,0:T(8,128)S(1)} %get-tuple-element.61) | copy-start | bytes 3145732
  264.4 95.4 %all-gather.9.cloned.1.call-start = ((), (), s32[]{:S(2)}) async-start(), calls=%async_computation.8 | async-start | bytes 2359296 | tf_op jit(solution)/shard_map/all_gather | solution.py:439
  267.6 127.4 %all-reduce.15.cloned.1.call-start = ((), (), s32[]{:S(2)}) async-start(), calls=%async_computation.10 | async-start | bytes 1048576 | tf_op jit(solution)/shard_map/psum | solution.py:292
  270.3 44.0 %copy-start.32 = (bf16[128,2,8,64]{0,3,2,1:T(8,128)(2,1)}, bf16[128,2,8,64]{0,3,2,1:T(8,128)(2,1)S(1)}, u32[]{:S(2)}) copy-start(bf16[128,2,8,64]{0,3,2,1:T(8,128)(2,1)S(1)} %copy.107) | copy-start | bytes 786436
  366.9 33.3 %copy-start.46 = (bf16[256,512]{1,0:T(8,128)(2,1)}, bf16[256,512]{1,0:T(8,128)(2,1)S(1)}, u32[]{:S(2)}) copy-start(bf16[256,512]{1,0:T(8,128)(2,1)S(1)} %reshape.398) | copy-start | bytes 786436
  369.5 62.3 %all-reduce.17.cloned.1.call-start = ((), (), s32[]{:S(2)}) async-start(), calls=%async_computation.11 | async-start | bytes 1048576 | tf_op jit(solution)/shard_map/psum | solution.py:292
  406.0 27.7 %copy-start.16 = (f32[256,1024]{1,0:T(8,128)S(1)}, f32[256,1024]{1,0:T(8,128)}, u32[]{:S(2)}) copy-start(f32[256,1024]{1,0:T(8,128)} %reshape.419) | copy-start | bytes 3145732
  406.0 66.1 %all-reduce.19.cloned.1.call-start = ((), (), s32[]{:S(2)}) async-start(), calls=%async_computation.12 | async-start | bytes 1048576 | tf_op jit(solution)/shard_map/psum | solution.py:295
  435.5 36.6 %copy-start.13 = (f32[256,1024]{1,0:T(8,128)}, f32[256,1024]{1,0:T(8,128)S(1)}, u32[]{:S(2)}) copy-start(f32[256,1024]{1,0:T(8,128)S(1)} %get-tuple-element.62) | copy-start | bytes 3145732
  446.3 97.3 %reduce-scatter.13.cloned.1.call-start = ((), (), s32[]{:S(2)}) async-start(), calls=%async_computation.16 | async-start | bytes 2359296
  486.7 6.7 copy-start.33
  499.4 88.2 %reduce-scatter.15.cloned.1.call-start = ((), (), s32[]{:S(2)}) async-start(), calls=%async_computation.17 | async-start | bytes 2359296
  510.3 109.6 %all-reduce.21.cloned.1.call-start = ((), (), s32[]{:S(2)}) async-start(), calls=%async_computation.13 | async-start | bytes 1048576 | tf_op jit(solution)/shard_map/psum | solution.py:295
  517.6 32.0 %copy-start.26 = (bf16[256,512]{1,0:T(8,128)(2,1)}, bf16[256,512]{1,0:T(8,128)(2,1)S(1)}, u32[]{:S(2)}) copy-start(bf16[256,512]{1,0:T(8,128)(2,1)S(1)} %reshape.401) | copy-start | bytes 786436
  588.8 8.0 copy-start.24
  592.1 30.6 %copy-start.54 = (f32[256]{0:T(256)S(1)}, f32[256]{0:T(256)}, u32[]{:S(2)}) copy-start(f32[256]{0:T(256)} %copy-done.53) | copy-start | bytes 3076
  596.8 64.2 %all-reduce.23.cloned.1.call-start = ((), (), s32[]{:S(2)}) async-start(), calls=%async_computation.14 | async-start | bytes 1048576 | tf_op jit(solution)/shard_map/psum | solution.py:295
  635.2 107.1 %reduce-scatter.19.cloned.1.call-start = ((), (), s32[]{:S(2)}) async-start(), calls=%async_computation.19 | async-start | bytes 2359296
  682.6 88.3 %reduce-scatter.17.cloned.1.call-start = ((), (), s32[]{:S(2)}) async-start(), calls=%async_computation.18 | async-start | bytes 2359296
  685.4 16.3 %slice-start = ((s8[8388608]{0:T(1024)(128)(4,1)}), s8[4194304]{0:T(1024)(128)(4,1)S(1)}, s32[]{:S(2)}) async-start(s8[8388608]{0:T(1024)(128)(4,1)} %bitcast.163), calls=%async_computation.20 | async-start | bytes 8388608
  691.4 6.6 copy-start.47
  691.4 10.2 %slice-start.1 = ((s8[8388608]{0:T(1024)(128)(4,1)}), s8[4194304]{0:T(1024)(128)(4,1)S(1)}, s32[]{:S(2)}) async-start(s8[8388608]{0:T(1024)(128)(4,1)} %bitcast.163), calls=%async_computation.21 | async-start | bytes 8388608
  711.0 6.2 copy-start.25
  711.0 6.3 copy-start.52
  711.0 6.4 copy-start.49
  715.2 168.2 %all-reduce.25.cloned.1.call-start = ((), (), s32[]{:S(2)}) async-start(), calls=%async_computation.15 | async-start | bytes 1048576 | tf_op jit(solution)/shard_map/psum | solution.py:295
  715.4 9.1 %slice-start.2 = ((s8[8388608]{0:T(1024)(128)(4,1)}), s8[4194304]{0:T(1024)(128)(4,1)S(1)}, s32[]{:S(2)}) async-start(s8[8388608]{0:T(1024)(128)(4,1)} %bitcast.165), calls=%async_computation.22 | async-start | bytes 8388608
  717.4 7.1 slice-start.3
  717.4 7.1 copy-start.9
  717.4 7.1 copy-start.42
  735.5 6.2 copy-start.11
  735.6 6.2 copy-start.19
  735.6 6.2 copy-start.45
  790.3 66.2 %copy-start.23 = (f32[256,1024]{1,0:T(8,128)S(1)}, f32[256,1024]{1,0:T(8,128)}, u32[]{:S(2)}) copy-start(f32[256,1024]{1,0:T(8,128)} %fusion.112) | copy-start | bytes 3145732
  853.8 6.9 copy-start.50
  (35 other events, 124.1 us)
Sparse Core Ops, SparseCore 0:
  88.9 44.1 all-gather.6
  135.2 46.2 all-gather.4
  191.3 25.3 all-reduce.10
  229.1 25.6 all-reduce.12
  264.6 46.7 all-gather.10
  313.3 46.4 all-gather.8
  369.6 25.3 all-reduce.14
  406.1 25.6 all-reduce.16
  446.4 25.6 all-reduce.18
  499.6 44.0 reduce-scatter.12
  546.2 41.4 reduce-scatter.14
  596.9 22.9 all-reduce.20
  635.3 25.6 all-reduce.22
  682.7 43.8 reduce-scatter.18
  729.0 41.8 reduce-scatter.16
  860.8 22.5 all-reduce.24
